TPU v7x, 256 devices: a whole 4x4x8 slice. The times are simulated.
256 devices in a mesh: dp: 8 (over x_lo, y), seq: 32 (over x_hi, z, core).
Axes of the slice: x: 4 (x_hi: 2, x_lo: 2; x = x_hi * 2 + x_lo), y: 4, z: 8, core: 2. Of those that a mesh axis runs over, the one named last changes fastest.
Arguments:
- queries: bfloat16 [32768, 2048], P(('dp', 'seq')), may hold values from -12 to 12
- key_rows: bfloat16 [32768, 2048], P(('dp', 'seq')), may hold values from -12 to 12
- value_rows: bfloat16 [32768, 2048], P(('dp', 'seq')), may hold values from -6 to 6
- document_ids: int32 [8, 4096], P('dp'), may hold values from 0 to 31, never falling along the last dimension, each value on 1 to 512 neighbouring positions
- link_lists: int32 [8, 32, 8], P('dp'), may hold values from 0 to 31, as said below
- block_keep: int32 [8, 32, 32], P('dp'), may hold values 0 or 1
- out_gain: float32 [2048], replicated, may hold values from 0.1 to 1.9
- cotangent: bfloat16 [32768, 2048], P(('dp', 'seq')), may hold values from -0.25 to 0.25
Outputs:
- attended: bfloat16 [32768, 2048], P(('dp', 'seq'))
- gain_grad: float32 [2048], P(('dp', 'seq'))
Inputs may be any that keep to these rules, and one draw needn't show every extreme that they name: `link_lists`: each target document lies within 3 documents of its source.
All inputs are finite; a program needn't handle non-finite values. No bound on the sum of `block_keep` on one device may be relied on, other than what follows from the above.
Results may differ from a plain program's by a relative error of at most 0.0035.
Values may be sent and summed in bfloat16 or wider, within the bound.
No kernel may reach another device: no remote copies, remote signals or barrier semaphores. Data moves between devices by JAX's collectives and lax.ppermute only.
A program may use at most 64 MiB of HBM per device.

v0:
```python
import math

import jax
import jax.numpy as jnp
from jax import lax
from jax.sharding import PartitionSpec as P

HEADS = 32
HDIM = 64
REACH = 3
BLK = 128


NEGATIVE_FILL = -1e30


def from_behind(shard, axis, by):
    peers = lax.axis_size(axis)
    return lax.ppermute(shard, axis, [(i, (i + by) % peers) for i in range(peers)])


def local(queries, key_rows, value_rows, document_ids, link_lists, block_keep, out_gain, cotangent):
    tokens_here = queries.shape[0]
    shards = lax.axis_size("seq")
    myself = lax.axis_index("seq")
    blocks_here = tokens_here // BLK
    score_scale = 1.0 / math.sqrt(HDIM)
    query_heads = queries.reshape(tokens_here, HEADS, HDIM)
    offsets = jnp.arange(tokens_here, dtype=jnp.int32)
    query_pos = myself * tokens_here + offsets
    documents = document_ids[0]
    query_docs = lax.dynamic_slice_in_dim(documents, myself * tokens_here, tokens_here, 0)
    query_links = link_lists[0][query_docs]
    query_keep = lax.dynamic_slice_in_dim(block_keep[0], myself * blocks_here, blocks_here, 0)

    def allowed_for(source):
        clipped = jnp.clip(source, 0, shards - 1)
        key_pos = source * tokens_here + offsets
        key_docs = lax.dynamic_slice_in_dim(documents, clipped * tokens_here, tokens_here, 0)
        in_window = jnp.abs(query_pos[:, None] - key_pos[None, :]) <= REACH * tokens_here
        same_doc = query_docs[:, None] == key_docs[None, :]
        linked = jnp.any(query_links[:, :, None] == key_docs[None, None, :], axis=1)
        block_bits = (
            lax.dynamic_slice_in_dim(query_keep, clipped * blocks_here, blocks_here, 1) == 1
        )
        expanded = jnp.repeat(jnp.repeat(block_bits, BLK, axis=0), BLK, axis=1)
        present = (source >= 0) & (source < shards)
        return present & in_window & (same_doc | linked & expanded)

    def absorb(carried, moving, source):
        keys_here = moving[0].reshape(tokens_here, HEADS, HDIM)
        values_here = moving[1].reshape(tokens_here, HEADS, HDIM)
        allowed = allowed_for(source)
        numerator, maxima, denominator = carried
        scores = (
            jnp.einsum("thd,uhd->htu", query_heads, keys_here, preferred_element_type=jnp.float32)
            * score_scale
        )
        masked = jnp.where(allowed[None], scores, NEGATIVE_FILL)
        new_max = jnp.maximum(maxima, jnp.max(masked, axis=-1))
        correction = jnp.exp(maxima - new_max)
        expo = jnp.where(allowed[None], jnp.exp(masked - new_max[..., None]), 0.0)
        new_denominator = denominator * correction + jnp.sum(expo, axis=-1)
        product = jnp.einsum(
            "htu,uhd->thd",
            expo.astype(jnp.bfloat16),
            values_here,
            preferred_element_type=jnp.float32,
        )
        new_numerator = numerator * jnp.transpose(correction)[:, :, None] + product
        return (new_numerator, new_max, new_denominator)

    carried = (
        jnp.zeros((tokens_here, HEADS, HDIM), jnp.float32),
        jnp.full((HEADS, tokens_here), NEGATIVE_FILL, jnp.float32),
        jnp.zeros((HEADS, tokens_here), jnp.float32),
    )
    carried = absorb(carried, (key_rows, value_rows), myself)
    moving = from_behind((key_rows, value_rows), "seq", -REACH)
    carried = absorb(carried, moving, myself + REACH)
    for hop_index in range(1, 2 * REACH + 1):
        moving = from_behind((moving[0], moving[1]), "seq", 1)
        if hop_index != REACH:
            carried = absorb(carried, moving, myself + REACH - hop_index)
    numerator, maxima, denominator = carried
    mixed = (numerator / jnp.transpose(denominator)[:, :, None]).reshape(tokens_here, HEADS * HDIM)
    attended = (out_gain * mixed).astype(jnp.bfloat16)
    local_terms = jnp.sum(mixed * cotangent.astype(jnp.float32), axis=0)
    gain_grad = lax.psum_scatter(local_terms, ("dp", "seq"), scatter_dimension=0, tiled=True)
    return (attended, gain_grad)


def solution(mesh):
    placed = (
        P(("dp", "seq"), None),
        P(("dp", "seq"), None),
        P(("dp", "seq"), None),
        P("dp", None),
        P("dp", None, None),
        P("dp", None, None),
        P(),
        P(("dp", "seq"), None),
    )
    return jax.shard_map(
        local,
        mesh=mesh,
        in_specs=placed,
        out_specs=(P(("dp", "seq"), None), P(("dp", "seq"))),
        check_vma=False,
    )
```

profile of v0, /device:TPU:1, one launch (start us, length us, event | category | flops | bytes accessed | tf_op | source)
XLA Modules:
  0.0 213.7 jit_solution(7257919064475032230)
XLA Ops:
  0.6 9.5 %collective-permute-start = (bf16[128,2048]{1,0:T(8,128)(2,1)}, bf16[128,2048]{1,0:T(8,128)(2,1)S(1)}, u32[]{:S(2)}, u32[]{:S(2)}) collective-permute-start(bf16[128,2048]{1,0:T(8,128)(2,1)} %param.9), channel_id=1, source_target_pairs={{0,29},{1,30},{2,31},{3,0},{4,1},{5,2},{6,3},{7,4},{8,5},{9,6},{10... | collective-permute-start | bytes 1572872 | tf_op jit(solution)/shard_map/ppermute | solution.py:19
  11.0 15.4 %collective-permute-done = bf16[128,2048]{1,0:T(8,128)(2,1)S(1)} collective-permute-done((bf16[128,2048]{1,0:T(8,128)(2,1)}, bf16[128,2048]{1,0:T(8,128)(2,1)S(1)}, u32[]{:S(2)}, u32[]{:S(2)}) %collective-permute-start) | collective-permute-done | bytes 524320 | tf_op jit(solution)/shard_map/ppermute | solution.py:19
  26.4 2.6 %collective-permute-start.2 = (bf16[128,2048]{1,0:T(8,128)(2,1)S(1)}, bf16[128,2048]{1,0:T(8,128)(2,1)S(1)}, u32[]{:S(2)}, u32[]{:S(2)}) collective-permute-start(bf16[128,2048]{1,0:T(8,128)(2,1)S(1)} %collective-permute-done), channel_id=1, source_target_pairs={{0,1},{1,2},{2,3},{3,4},{4,5},{5,6},{6,7},{7,8},{8,9},{9,10},{10,1... | collective-permute-start | bytes 1572872 | tf_op jit(solution)/shard_map/ppermute | solution.py:19
  29.1 15.2 %collective-permute-done.1 = bf16[128,2048]{1,0:T(8,128)(2,1)S(1)} collective-permute-done((bf16[128,2048]{1,0:T(8,128)(2,1)}, bf16[128,2048]{1,0:T(8,128)(2,1)S(1)}, u32[]{:S(2)}, u32[]{:S(2)}) %collective-permute-start.1) | collective-permute-done | bytes 524320 | tf_op jit(solution)/shard_map/ppermute | solution.py:19
  61.8 2.5 %collective-permute-start.8 = (bf16[128,2048]{1,0:T(8,128)(2,1)}, bf16[128,2048]{1,0:T(8,128)(2,1)}, u32[]{:S(2)}, u32[]{:S(2)}) collective-permute-start(bf16[128,2048]{1,0:T(8,128)(2,1)} %collective-permute-done.5), channel_id=1, source_target_pairs={{0,1},{1,2},{2,3},{3,4},{4,5},{5,6},{6,7},{7,8},{8,9},{9,10},{10,1... | collective-permute-start | bytes 1572872 | tf_op jit(solution)/shard_map/ppermute | solution.py:19
  64.6 2.8 %collective-permute-done.6 = bf16[128,2048]{1,0:T(8,128)(2,1)} collective-permute-done((bf16[128,2048]{1,0:T(8,128)(2,1)}, bf16[128,2048]{1,0:T(8,128)(2,1)}, u32[]{:S(2)}, u32[]{:S(2)}) %collective-permute-start.6) | collective-permute-done | bytes 524320 | tf_op jit(solution)/shard_map/ppermute | solution.py:19
  67.4 2.5 %collective-permute-start.7 = (bf16[128,2048]{1,0:T(8,128)(2,1)}, bf16[128,2048]{1,0:T(8,128)(2,1)}, u32[]{:S(2)}, u32[]{:S(2)}) collective-permute-start(bf16[128,2048]{1,0:T(8,128)(2,1)} %collective-permute-done.6), channel_id=1, source_target_pairs={{0,1},{1,2},{2,3},{3,4},{4,5},{5,6},{6,7},{7,8},{8,9},{9,10},{10,1... | collective-permute-start | bytes 1572872 | tf_op jit(solution)/shard_map/ppermute | solution.py:19
  73.1 2.4 %collective-permute-start.9 = (bf16[128,2048]{1,0:T(8,128)(2,1)}, bf16[128,2048]{1,0:T(8,128)(2,1)}, u32[]{:S(2)}, u32[]{:S(2)}) collective-permute-start(bf16[128,2048]{1,0:T(8,128)(2,1)} %collective-permute-done.8), channel_id=1, source_target_pairs={{0,1},{1,2},{2,3},{3,4},{4,5},{5,6},{6,7},{7,8},{8,9},{9,10},{10,1... | collective-permute-start | bytes 1572872 | tf_op jit(solution)/shard_map/ppermute | solution.py:19
  77.1 2.1 copy.102
  79.1 2.1 copy.103
  81.2 2.9 %fusion.2 = (f32[32,128]{1,0:T(8,128)S(1)}, f32[32,128,128]{1,2,0:T(8,128)}) fusion(pred[128,128]{0,1:T(8,128)(4,1)S(1)} %copy.101, bf16[128,32,64]{0,2,1:T(8,128)(2,1)S(1)} %bitcast.221, bf16[128,32,64]{0,2,1:T(8,128)(2,1)} %bitcast.233), kind=kOutput, calls=%fused_computation.17 | convolution fusion | flops 68677632 | bytes 3178496 | tf_op jit(solution)/shard_map/thd,uhd->htu/dot_general | solution.py:56
  84.1 2.1 copy.106
  86.2 2.0 copy.107
  88.2 2.9 %fusion.3 = (f32[32,128]{1,0:T(8,128)S(1)}, f32[32,128,128]{1,2,0:T(8,128)}) fusion(pred[128,128]{0,1:T(8,128)(4,1)S(1)} %copy.105, bf16[128,32,64]{0,2,1:T(8,128)(2,1)S(1)} %bitcast.222, bf16[128,32,64]{0,2,1:T(8,128)(2,1)} %bitcast.234), kind=kOutput, calls=%fused_computation.18 | convolution fusion | flops 68677632 | bytes 3178496 | tf_op jit(solution)/shard_map/thd,uhd->htu/dot_general | solution.py:56
  91.1 2.0 copy.110
  93.1 2.0 copy.111
  95.2 2.9 %fusion.4 = (f32[32,128]{1,0:T(8,128)S(1)}, f32[32,128,128]{1,2,0:T(8,128)}) fusion(pred[128,128]{0,1:T(8,128)(4,1)S(1)} %copy.109, bf16[128,32,64]{0,2,1:T(8,128)(2,1)S(1)} %bitcast.223, bf16[128,32,64]{0,2,1:T(8,128)(2,1)} %bitcast.236), kind=kOutput, calls=%fused_computation.19 | convolution fusion | flops 68677632 | bytes 3178496 | tf_op jit(solution)/shard_map/thd,uhd->htu/dot_general | solution.py:56
  98.1 2.0 copy.114
  100.2 2.1 copy.115
  103.4 2.9 %fusion.5 = (f32[32,128]{1,0:T(8,128)S(1)}, f32[32,128,128]{1,2,0:T(8,128)}) fusion(pred[128,128]{0,1:T(8,128)(4,1)S(1)} %copy.113, bf16[128,32,64]{0,2,1:T(8,128)(2,1)S(1)} %bitcast.224, bf16[128,32,64]{0,2,1:T(8,128)(2,1)} %bitcast.237), kind=kOutput, calls=%fused_computation.20 | convolution fusion | flops 68677632 | bytes 3178496 | tf_op jit(solution)/shard_map/thd,uhd->htu/dot_general | solution.py:56
  106.3 2.0 copy.118
  122.6 2.0 copy.119
  124.7 2.1 fusion.22
  128.8 84.3 %all-reduce = f32[2048]{0:T(1024)S(1)} all-reduce(f32[2048]{0:T(1024)S(1)} %get-tuple-element.21), channel_id=2, replica_groups=mesh['dp'=8,'seq'=32] {'dp','seq'}, use_global_device_ids=true, to_apply=%region_22.23.clone | all-reduce | flops 2048 | bytes 16384
  (105 shorter events, 36.7 us)
Async XLA Ops:
  0.6 53.9 %copy-start.11 = (bf16[128,2048]{1,0:T(8,128)(2,1)S(1)}, bf16[128,2048]{1,0:T(8,128)(2,1)}, u32[]{:S(2)}) copy-start(bf16[128,2048]{1,0:T(8,128)(2,1)} %param.10) | copy-start | bytes 1572868
  0.6 55.0 %copy-start.12 = (bf16[128,2048]{1,0:T(8,128)(2,1)S(1)}, bf16[128,2048]{1,0:T(8,128)(2,1)}, u32[]{:S(2)}) copy-start(bf16[128,2048]{1,0:T(8,128)(2,1)} %param.8) | copy-start | bytes 1572868
  0.6 25.8 %collective-permute-start = (bf16[128,2048]{1,0:T(8,128)(2,1)}, bf16[128,2048]{1,0:T(8,128)(2,1)S(1)}, u32[]{:S(2)}, u32[]{:S(2)}) collective-permute-start(bf16[128,2048]{1,0:T(8,128)(2,1)} %param.9), channel_id=1, source_target_pairs={{0,29},{1,30},{2,31},{3,0},{4,1},{5,2},{6,3},{7,4},{8,5},{9,6},{10... | collective-permute-start | bytes 1572872 | tf_op jit(solution)/shard_map/ppermute | solution.py:19
  10.2 34.1 %collective-permute-start.1 = (bf16[128,2048]{1,0:T(8,128)(2,1)}, bf16[128,2048]{1,0:T(8,128)(2,1)S(1)}, u32[]{:S(2)}, u32[]{:S(2)}) collective-permute-start(bf16[128,2048]{1,0:T(8,128)(2,1)} %param.10), channel_id=1, source_target_pairs={{0,29},{1,30},{2,31},{3,0},{4,1},{5,2},{6,3},{7,4},{8,5},{9,6},{10... | collective-permute-start | bytes 1572872 | tf_op jit(solution)/shard_map/ppermute | solution.py:19
  26.4 19.3 %collective-permute-start.2 = (bf16[128,2048]{1,0:T(8,128)(2,1)S(1)}, bf16[128,2048]{1,0:T(8,128)(2,1)S(1)}, u32[]{:S(2)}, u32[]{:S(2)}) collective-permute-start(bf16[128,2048]{1,0:T(8,128)(2,1)S(1)} %collective-permute-done), channel_id=1, source_target_pairs={{0,1},{1,2},{2,3},{3,4},{4,5},{5,6},{6,7},{7,8},{8,9},{9,10},{10,1... | collective-permute-start | bytes 1572872 | tf_op jit(solution)/shard_map/ppermute | solution.py:19
  44.3 8.9 %copy-start.14 = (bf16[128,2048]{1,0:T(8,128)(2,1)}, bf16[128,2048]{1,0:T(8,128)(2,1)S(1)}, u32[]{:S(2)}) copy-start(bf16[128,2048]{1,0:T(8,128)(2,1)S(1)} %collective-permute-done.1) | copy-start | bytes 1572868
  44.3 7.8 %collective-permute-start.3 = (bf16[128,2048]{1,0:T(8,128)(2,1)S(1)}, bf16[128,2048]{1,0:T(8,128)(2,1)}, u32[]{:S(2)}, u32[]{:S(2)}) collective-permute-start(bf16[128,2048]{1,0:T(8,128)(2,1)S(1)} %collective-permute-done.1), channel_id=1, source_target_pairs={{0,1},{1,2},{2,3},{3,4},{4,5},{5,6},{6,7},{7,8},{8,9},{9,10},{10,1... | collective-permute-start | bytes 1572872 | tf_op jit(solution)/shard_map/ppermute | solution.py:19
  45.8 10.2 %copy-start.13 = (bf16[128,2048]{1,0:T(8,128)(2,1)}, bf16[128,2048]{1,0:T(8,128)(2,1)S(1)}, u32[]{:S(2)}) copy-start(bf16[128,2048]{1,0:T(8,128)(2,1)S(1)} %collective-permute-done.2) | copy-start | bytes 1572868
  45.8 12.1 %collective-permute-start.4 = (bf16[128,2048]{1,0:T(8,128)(2,1)S(1)}, bf16[128,2048]{1,0:T(8,128)(2,1)}, u32[]{:S(2)}, u32[]{:S(2)}) collective-permute-start(bf16[128,2048]{1,0:T(8,128)(2,1)S(1)} %collective-permute-done.2), channel_id=1, source_target_pairs={{0,1},{1,2},{2,3},{3,4},{4,5},{5,6},{6,7},{7,8},{8,9},{9,10},{10,1... | collective-permute-start | bytes 1572872 | tf_op jit(solution)/shard_map/ppermute | solution.py:19
  52.1 9.6 %collective-permute-start.5 = (bf16[128,2048]{1,0:T(8,128)(2,1)}, bf16[128,2048]{1,0:T(8,128)(2,1)}, u32[]{:S(2)}, u32[]{:S(2)}) collective-permute-start(bf16[128,2048]{1,0:T(8,128)(2,1)} %collective-permute-done.3), channel_id=1, source_target_pairs={{0,1},{1,2},{2,3},{3,4},{4,5},{5,6},{6,7},{7,8},{8,9},{9,10},{10,1... | collective-permute-start | bytes 1572872 | tf_op jit(solution)/shard_map/ppermute | solution.py:19
  57.9 9.5 %collective-permute-start.6 = (bf16[128,2048]{1,0:T(8,128)(2,1)}, bf16[128,2048]{1,0:T(8,128)(2,1)}, u32[]{:S(2)}, u32[]{:S(2)}) collective-permute-start(bf16[128,2048]{1,0:T(8,128)(2,1)} %collective-permute-done.4), channel_id=1, source_target_pairs={{0,1},{1,2},{2,3},{3,4},{4,5},{5,6},{6,7},{7,8},{8,9},{9,10},{10,1... | collective-permute-start | bytes 1572872 | tf_op jit(solution)/shard_map/ppermute | solution.py:19
  61.8 11.3 %collective-permute-start.8 = (bf16[128,2048]{1,0:T(8,128)(2,1)}, bf16[128,2048]{1,0:T(8,128)(2,1)}, u32[]{:S(2)}, u32[]{:S(2)}) collective-permute-start(bf16[128,2048]{1,0:T(8,128)(2,1)} %collective-permute-done.5), channel_id=1, source_target_pairs={{0,1},{1,2},{2,3},{3,4},{4,5},{5,6},{6,7},{7,8},{8,9},{9,10},{10,1... | collective-permute-start | bytes 1572872 | tf_op jit(solution)/shard_map/ppermute | solution.py:19
  67.4 13.8 %collective-permute-start.7 = (bf16[128,2048]{1,0:T(8,128)(2,1)}, bf16[128,2048]{1,0:T(8,128)(2,1)}, u32[]{:S(2)}, u32[]{:S(2)}) collective-permute-start(bf16[128,2048]{1,0:T(8,128)(2,1)} %collective-permute-done.6), channel_id=1, source_target_pairs={{0,1},{1,2},{2,3},{3,4},{4,5},{5,6},{6,7},{7,8},{8,9},{9,10},{10,1... | collective-permute-start | bytes 1572872 | tf_op jit(solution)/shard_map/ppermute | solution.py:19
  69.9 2.9 %copy-start.15 = (bf16[128,2048]{1,0:T(8,128)(2,1)S(1)}, bf16[128,2048]{1,0:T(8,128)(2,1)}, u32[]{:S(2)}) copy-start(bf16[128,2048]{1,0:T(8,128)(2,1)} %copy-done.14) | copy-start | bytes 1572868
  73.1 15.1 %collective-permute-start.9 = (bf16[128,2048]{1,0:T(8,128)(2,1)}, bf16[128,2048]{1,0:T(8,128)(2,1)}, u32[]{:S(2)}, u32[]{:S(2)}) collective-permute-start(bf16[128,2048]{1,0:T(8,128)(2,1)} %collective-permute-done.8), channel_id=1, source_target_pairs={{0,1},{1,2},{2,3},{3,4},{4,5},{5,6},{6,7},{7,8},{8,9},{9,10},{10,1... | collective-permute-start | bytes 1572872 | tf_op jit(solution)/shard_map/ppermute | solution.py:19
  81.2 14.0 %collective-permute-start.10 = (bf16[128,2048]{1,0:T(8,128)(2,1)}, bf16[128,2048]{1,0:T(8,128)(2,1)}, u32[]{:S(2)}, u32[]{:S(2)}) collective-permute-start(bf16[128,2048]{1,0:T(8,128)(2,1)} %collective-permute-done.7), channel_id=1, source_target_pairs={{0,1},{1,2},{2,3},{3,4},{4,5},{5,6},{6,7},{7,8},{8,9},{9,10},{10,1... | collective-permute-start | bytes 1572872 | tf_op jit(solution)/shard_map/ppermute | solution.py:19
  88.2 12.0 %collective-permute-start.11 = (bf16[128,2048]{1,0:T(8,128)(2,1)}, bf16[128,2048]{1,0:T(8,128)(2,1)}, u32[]{:S(2)}, u32[]{:S(2)}) collective-permute-start(bf16[128,2048]{1,0:T(8,128)(2,1)} %collective-permute-done.9), channel_id=1, source_target_pairs={{0,1},{1,2},{2,3},{3,4},{4,5},{5,6},{6,7},{7,8},{8,9},{9,10},{10,1... | collective-permute-start | bytes 1572872 | tf_op jit(solution)/shard_map/ppermute | solution.py:19
  95.2 11.1 %collective-permute-start.12 = (bf16[128,2048]{1,0:T(8,128)(2,1)}, bf16[128,2048]{1,0:T(8,128)(2,1)}, u32[]{:S(2)}, u32[]{:S(2)}) collective-permute-start(bf16[128,2048]{1,0:T(8,128)(2,1)} %collective-permute-done.10), channel_id=1, source_target_pairs={{0,1},{1,2},{2,3},{3,4},{4,5},{5,6},{6,7},{7,8},{8,9},{9,10},{10,1... | collective-permute-start | bytes 1572872 | tf_op jit(solution)/shard_map/ppermute | solution.py:19
  102.2 20.4 %collective-permute-start.13 = (bf16[128,2048]{1,0:T(8,128)(2,1)}, bf16[128,2048]{1,0:T(8,128)(2,1)}, u32[]{:S(2)}, u32[]{:S(2)}) collective-permute-start(bf16[128,2048]{1,0:T(8,128)(2,1)} %collective-permute-done.11), channel_id=1, source_target_pairs={{0,1},{1,2},{2,3},{3,4},{4,5},{5,6},{6,7},{7,8},{8,9},{9,10},{10,1... | collective-permute-start | bytes 1572872 | tf_op jit(solution)/shard_map/ppermute | solution.py:19
  108.4 1.8 copy-start.4
  110.1 5.3 %copy-start.5 = (f32[32,128,128]{1,2,0:T(8,128)}, f32[32,128,128]{1,2,0:T(8,128)S(1)}, u32[]{:S(2)}) copy-start(f32[32,128,128]{1,2,0:T(8,128)S(1)} %get-tuple-element.48) | copy-start | bytes 6291460
  110.1 2.3 %copy-start = (f32[32,128,128]{1,2,0:T(8,128)S(1)}, f32[32,128,128]{1,2,0:T(8,128)}, u32[]{:S(2)}) copy-start(f32[32,128,128]{1,2,0:T(8,128)} %get-tuple-element.56) | copy-start | bytes 6291460
  110.7 2.4 %copy-start.1 = (f32[32,128,128]{1,2,0:T(8,128)S(1)}, f32[32,128,128]{1,2,0:T(8,128)}, u32[]{:S(2)}) copy-start(f32[32,128,128]{1,2,0:T(8,128)} %get-tuple-element.54) | copy-start | bytes 6291460
  120.9 3.8 %copy-start.6 = (f32[32,128,128]{1,2,0:T(8,128)S(1)}, f32[32,128,128]{1,2,0:T(8,128)}, u32[]{:S(2)}) copy-start(f32[32,128,128]{1,2,0:T(8,128)} %copy-done.5) | copy-start | bytes 6291460
  (9 other events, 10.9 us)
where the time goes:
time: 215 us; the launch traced here: 214 us
  blocking collectives  84.3 us (39%)
  waiting for transfers between devices  35.2 us (16%)
  local copies, waits for them, and re-layouts  33.8 us (16%)
  matrix products  24.3 us (11%)
  starting transfers between devices  23.4 us (11%)
  other arithmetic  7.07 us (3%)
  between operations  5.64 us (3%)
    unnamed x1, blocking collectives  84.3 us
    ppermute x14, waiting for transfers between devices, from_behind(): lax.ppermute(shard, axis, [(i, (i + by) % peers) for i in range(peers)])  35.2 us
    ppermute x14, starting transfers between devices, from_behind(): lax.ppermute(shard, axis, [(i, (i + by) % peers) for i in range(peers)])  23.4 us
    ppermute x12, local copies, waits for them, and re-layouts, from_behind(): lax.ppermute(shard, axis, [(i, (i + by) % peers) for i in range(peers)])  21.8 us
    dot_general x7, matrix products, absorb(): jnp.einsum('thd,uhd->htu', query_heads, keys_here, preferred_element_type...  16.8 us
    unnamed x43, local copies, waits for them, and re-layouts  7.78 us
    dot_general x7, matrix products, absorb(): jnp.einsum('htu,uhd->thd', expo.astype(jnp.bfloat16), values_here, prefer...  7.55 us
  transfers between devices with their start and end apart: 14, of which 4 were waited for; matrix products, arithmetic and copies ran while one was open for 26% of the time, Pallas kernels for 0%

commit v1 on v0

v1 whole, which is shorter than its diff:
```python
import functools
import math

import jax
import jax.numpy as jnp
from jax import lax
from jax.experimental import pallas as pl
from jax.experimental.pallas import tpu as pltpu
from jax.sharding import PartitionSpec as P

HEADS = 32
HDIM = 64
REACH = 3
BLK = 128
HALF = HEADS * HDIM // 2
PAIRS = HALF // 128
NEGATIVE_FILL = -1e30
AXES = ("dp", "seq")


def prep_kernel(core_ref, a_own, b_own, a_other, b_other, own_ref, send_ref):
    own_ref[:BLK] = a_own[...]
    own_ref[BLK:] = b_own[...]
    send_ref[:BLK] = a_other[...]
    send_ref[BLK:] = b_other[...]


def split_heads(core, a, b):
    steps = 2
    width = HALF // steps
    mine = pl.BlockSpec((BLK, width), lambda i, c: (0, c[0] * steps + i))
    others = pl.BlockSpec((BLK, width), lambda i, c: (0, (1 - c[0]) * steps + i))
    out = pl.BlockSpec((2 * BLK, width), lambda i, c: (0, i))
    shape = jax.ShapeDtypeStruct((2 * BLK, HALF), a.dtype)
    return pl.pallas_call(
        prep_kernel,
        grid_spec=pltpu.PrefetchScalarGridSpec(
            num_scalar_prefetch=1, grid=(steps,), in_specs=[mine, mine, others, others], out_specs=[out, out]
        ),
        out_shape=[shape, shape],
        cost_estimate=pl.CostEstimate(flops=0, bytes_accessed=4 << 20, transcendentals=0),
    )(core, a, b, a, b)


OWN, SIB, R1, R2, R3, R4, R5, R6 = range(8)
TILES = (
    [(q, k) for q in (OWN, SIB) for k in (OWN, SIB)]
    + [(q, k) for q in (OWN, SIB) for k in (R1, R2)]
    + [(q, k) for q in (OWN, SIB) for k in (R3, R4)]
    + [(SIB, R5), (OWN, R6)]
)


def mask_kernel(blocks_ref, keep_ref, docs_ref, links_ref, bias_ref):
    docs_in_pack = links_ref.shape[0]
    nblk = docs_ref.shape[1] // BLK
    target = lax.broadcasted_iota(jnp.int32, (docs_in_pack, docs_in_pack), 1)
    source = lax.broadcasted_iota(jnp.int32, (docs_in_pack, docs_in_pack), 0)
    linked = target == links_ref[:, 0:1]
    for at in range(1, links_ref.shape[1]):
        linked = linked | (target == links_ref[:, at : at + 1])
    table = jnp.where(source == target, 2.0, 0.0) + jnp.where(linked, 1.0, 0.0)
    table = table.astype(jnp.bfloat16)

    def one_hot(block):
        at = pl.multiple_of(jnp.clip(block, 0, nblk - 1) * BLK, BLK)
        row = docs_ref[:, pl.ds(at, BLK)]
        rows = lax.broadcasted_iota(jnp.int32, (docs_in_pack, BLK), 0)
        return jnp.where(rows == row, 1.0, 0.0).astype(jnp.bfloat16)

    hots = [one_hot(blocks_ref[place]) for place in range(8)]
    related = [
        lax.dot_general(table, hots[q], (((0,), (0,)), ((), ())), preferred_element_type=jnp.float32).astype(jnp.bfloat16)
        for q in (OWN, SIB)
    ]
    key_at = lax.broadcasted_iota(jnp.int32, (BLK, BLK), 0)
    query_at = lax.broadcasted_iota(jnp.int32, (BLK, BLK), 1)
    apart = query_at - key_at
    for tile, (q, k) in enumerate(TILES):
        query_block, key_block = blocks_ref[q], blocks_ref[k]
        present = (key_block >= 0) & (key_block < nblk)
        kept = keep_ref[query_block * nblk + jnp.clip(key_block, 0, nblk - 1)] == 1
        least = jnp.where(present, jnp.where(kept, 0.5, 1.5), 9.0)
        relation = lax.dot_general(hots[k], related[q], (((0,), (0,)), ((), ())), preferred_element_type=jnp.float32)
        distance = apart + (query_block - key_block) * BLK
        allowed = (relation > least) & (jnp.abs(distance) <= REACH * BLK)
        bias_ref[tile * BLK : (tile + 1) * BLK] = jnp.where(allowed, 0.0, NEGATIVE_FILL)


def masks(blocks, keep, docs, links):
    whole = lambda shape: pl.BlockSpec(shape, lambda i, *_: (0,) * len(shape))
    return pl.pallas_call(
        mask_kernel,
        grid_spec=pltpu.PrefetchScalarGridSpec(
            num_scalar_prefetch=2,
            grid=(1,),
            in_specs=[whole(docs.shape), whole(links.shape)],
            out_specs=whole((len(TILES) * BLK, BLK)),
        ),
        out_shape=jax.ShapeDtypeStruct((len(TILES) * BLK, BLK), jnp.float32),
        cost_estimate=pl.CostEstimate(flops=1 << 20, bytes_accessed=2 << 20, transcendentals=0),
    )(blocks, keep, docs, links)


def absorb(query, keys, values, bias, state):
    low = lax.broadcasted_iota(jnp.int32, query.shape, 1) < HDIM
    scaled = query * jnp.bfloat16(1.0 / math.sqrt(HDIM))
    nothing = jnp.zeros_like(scaled)
    both = jnp.concatenate([jnp.where(low, scaled, nothing), jnp.where(low, nothing, scaled)], axis=0)
    scores = lax.dot_general(keys, both, (((1,), (1,)), ((), ())), preferred_element_type=jnp.float32)
    scores = scores + jnp.concatenate([bias, bias], axis=1)
    largest = jnp.max(scores, axis=0, keepdims=True)
    if state is not None:
        largest = jnp.maximum(state[0], largest)
    expo = jnp.exp(scores - largest)
    totals = jnp.sum(expo, axis=0, keepdims=True)
    sums = lax.dot_general(
        values, expo.astype(jnp.bfloat16), (((0,), (0,)), ((), ())), preferred_element_type=jnp.float32
    )
    folded = jnp.concatenate([sums[:HDIM, :BLK], sums[HDIM:, BLK:]], axis=0)
    if state is not None:
        shrink = jnp.exp(state[0] - largest)
        totals = totals + state[1] * shrink
        folded = folded + state[2] * spread(shrink)
    return largest, totals, folded


def spread(row):
    first = jnp.broadcast_to(row[:, :BLK], (HDIM, BLK))
    second = jnp.broadcast_to(row[:, BLK:], (HDIM, BLK))
    return jnp.concatenate([first, second], axis=0)


def put_state(rows_ref, sums_ref, state):
    rows_ref[0:1] = state[0]
    rows_ref[1:2] = state[1]
    sums_ref[...] = state[2]


def first_kernel(bias_ref, qc_own, qc_sib, kv_a, kv_b, rows_own, sums_own, rows_sib, sums_sib):
    keys = jnp.concatenate([kv_a[:BLK], kv_b[:BLK]], axis=0)
    values = jnp.concatenate([kv_a[BLK:], kv_b[BLK:]], axis=0)
    put_state(rows_own, sums_own, absorb(qc_own[:BLK], keys, values, bias_ref[: 2 * BLK], None))
    put_state(rows_sib, sums_sib, absorb(qc_sib[:BLK], keys, values, bias_ref[2 * BLK :], None))


def middle_kernel(bias_ref, qc_own, qc_sib, kv_a, kv_b, ro, so, rs, ss, rows_own, sums_own, rows_sib, sums_sib):
    keys = jnp.concatenate([kv_a[:BLK], kv_b[:BLK]], axis=0)
    values = jnp.concatenate([kv_a[BLK:], kv_b[BLK:]], axis=0)
    state = (ro[0:1], ro[1:2], so[...])
    put_state(rows_own, sums_own, absorb(qc_own[:BLK], keys, values, bias_ref[: 2 * BLK], state))
    state = (rs[0:1], rs[1:2], ss[...])
    put_state(rows_sib, sums_sib, absorb(qc_sib[:BLK], keys, values, bias_ref[2 * BLK :], state))


def finish(state, gain, cotangent):
    mixed = jnp.transpose(state[2] / spread(state[1]))
    attended = (gain * mixed).astype(jnp.bfloat16)
    terms = jnp.sum(mixed * cotangent.astype(jnp.float32), axis=0, keepdims=True)
    return attended, terms


def sib_kernel(core_ref, bias_ref, qc, kv, rows, sums, gain_ref, att_ref, terms_ref):
    state = absorb(qc[:BLK], kv[:BLK], kv[BLK:], bias_ref[...], (rows[0:1], rows[1:2], sums[...]))
    att_ref[...], terms = finish(state, gain_ref[...], qc[BLK:])
    terms_ref[...] = jnp.broadcast_to(terms, terms_ref.shape)


def own_kernel(core_ref, bias_ref, qc, kv, rows, sums, gain_ref, terms_in, back, out_ref, terms_ref):
    state = absorb(qc[:BLK], kv[:BLK], kv[BLK:], bias_ref[...], (rows[0:1], rows[1:2], sums[...]))
    attended, terms = finish(state, gain_ref[...], qc[BLK:])
    core = core_ref[0]
    at = pl.program_id(0)
    out_ref[:, pl.ds(pl.multiple_of(core * HALF + at * BLK, BLK), BLK)] = attended
    out_ref[:, pl.ds(pl.multiple_of((1 - core) * HALF + at * BLK, BLK), BLK)] = back[...]

    @pl.when(at == 0)
    def _():
        terms_ref[...] = jnp.zeros_like(terms_ref)

    terms_ref[pl.ds(core * PAIRS + at, 1), :] = terms + terms_in[0:1]


ROWS = pl.BlockSpec((8, 2 * BLK), lambda j, *_: (j, 0))
SUMS = pl.BlockSpec((BLK, BLK), lambda j, *_: (j, 0))
COLS = pl.BlockSpec((2 * BLK, BLK), lambda j, *_: (0, j))
ONE = pl.BlockSpec((BLK, BLK), lambda j, *_: (0, j))
STATE = [
    jax.ShapeDtypeStruct((PAIRS * 8, 2 * BLK), jnp.float32),
    jax.ShapeDtypeStruct((PAIRS * BLK, BLK), jnp.float32),
]


def bias_at(tiles, place):
    return pl.BlockSpec((tiles * BLK, BLK), lambda j, *_: (place, 0))


def cost(tiles):
    return pl.CostEstimate(
        flops=tiles * 16 * 4 * BLK * BLK * HDIM, bytes_accessed=4 << 20, transcendentals=tiles * 16 * BLK * BLK
    )


def first(bias, qc_own, qc_sib, kv_a, kv_b):
    return pl.pallas_call(
        first_kernel,
        grid=(PAIRS,),
        in_specs=[bias_at(4, 0), COLS, COLS, COLS, COLS],
        out_specs=[ROWS, SUMS, ROWS, SUMS],
        out_shape=STATE + STATE,
        cost_estimate=cost(4),
    )(bias, qc_own, qc_sib, kv_a, kv_b)


def middle(place, bias, qc_own, qc_sib, kv_a, kv_b, state):
    return pl.pallas_call(
        middle_kernel,
        grid=(PAIRS,),
        in_specs=[bias_at(4, place), COLS, COLS, COLS, COLS, ROWS, SUMS, ROWS, SUMS],
        out_specs=[ROWS, SUMS, ROWS, SUMS],
        out_shape=STATE + STATE,
        cost_estimate=cost(4),
    )(bias, qc_own, qc_sib, kv_a, kv_b, *state)


def last_sib(core, bias, qc, kv, rows, sums, gain):
    return pl.pallas_call(
        sib_kernel,
        grid_spec=pltpu.PrefetchScalarGridSpec(
            num_scalar_prefetch=1,
            grid=(PAIRS,),
            in_specs=[bias_at(1, 12), COLS, COLS, ROWS, SUMS, pl.BlockSpec((1, BLK), lambda j, c: (0, c[0] * PAIRS + j))],
            out_specs=[ONE, pl.BlockSpec((8, BLK), lambda j, c: (j, 0))],
        ),
        out_shape=[
            jax.ShapeDtypeStruct((BLK, HALF), jnp.bfloat16),
            jax.ShapeDtypeStruct((PAIRS * 8, BLK), jnp.float32),
        ],
        cost_estimate=cost(1),
    )(core, bias, qc, kv, rows, sums, gain)


def last_own(core, bias, qc, kv, rows, sums, gain, terms, back):
    return pl.pallas_call(
        own_kernel,
        grid_spec=pltpu.PrefetchScalarGridSpec(
            num_scalar_prefetch=1,
            grid=(PAIRS,),
            in_specs=[
                bias_at(1, 13),
                COLS,
                COLS,
                ROWS,
                SUMS,
                pl.BlockSpec((1, BLK), lambda j, c: (0, c[0] * PAIRS + j)),
                pl.BlockSpec((8, BLK), lambda j, c: (j, 0)),
                ONE,
            ],
            out_specs=[
                pl.BlockSpec((BLK, 2 * HALF), lambda j, c: (0, 0)),
                pl.BlockSpec((2 * PAIRS, BLK), lambda j, c: (0, 0)),
            ],
        ),
        out_shape=[
            jax.ShapeDtypeStruct((BLK, 2 * HALF), jnp.bfloat16),
            jax.ShapeDtypeStruct((2 * PAIRS, BLK), jnp.float32),
        ],
        cost_estimate=cost(1),
    )(core, bias, qc, kv, rows, sums, gain, terms, back)


def rotations(groups, shards):
    onward = []
    for group in range(groups):
        for place in range(shards):
            chip, core = divmod(place, 2)
            there = chip + (1 if core == 1 else -1)
            target = there * 2 + core if 0 <= there < shards // 2 else chip * 2 + 1 - core
            onward.append((group * shards + place, group * shards + target))
    return onward, [(target, source) for source, target in onward]


def after(value, *others):
    return lax.optimization_barrier((value, *others))[0]


def local(queries, key_rows, value_rows, document_ids, link_lists, block_keep, out_gain, cotangent):
    groups, shards = lax.axis_size("dp"), lax.axis_size("seq")
    place = lax.axis_index("seq")
    chip, core = place // 2, place % 2
    toward = 1 - 2 * core
    chips = jnp.stack([chip, chip, chip + toward, chip - toward, chip - toward, chip + toward, chip + 2 * toward, chip - 2 * toward])
    cores = jnp.stack([core, 1 - core, core, 1 - core, core, 1 - core, core, 1 - core])
    blocks = jnp.where((chips >= 0) & (chips < shards // 2), 2 * chips + cores, -1).astype(jnp.int32)
    core_at = core.reshape(1).astype(jnp.int32)
    onward, backward = rotations(groups, shards)
    siblings = [(i, i ^ 1) for i in range(groups * shards)]
    move = lambda value, pairs: lax.ppermute(value, AXES, pairs)
    gain = out_gain.reshape(1, -1)

    kv_own, kv_send = split_heads(core_at, key_rows, value_rows)
    kv_sib = move(kv_send, siblings)
    r1 = move(kv_own, onward)
    r2 = move(kv_sib, backward)
    r3 = move(after(kv_own, r1), backward)
    r5 = move(after(r1, r2), onward)
    r4 = move(after(kv_sib, r3), onward)
    r6 = move(after(r2, r5), backward)

    qc_own, qc_send = split_heads(core_at, queries, cotangent)
    qc_sib = move(qc_send, siblings)
    bias = masks(blocks, block_keep.reshape(-1), document_ids, link_lists[0])

    state = first(bias, qc_own, qc_sib, kv_own, kv_sib)
    state = middle(1, bias, qc_own, qc_sib, r1, r2, state)
    state = middle(2, bias, qc_own, qc_sib, r3, r4, state)
    att_sib, terms = last_sib(core_at, bias, qc_sib, r5, state[2], state[3], gain)
    back = move(att_sib, siblings)
    attended, terms = last_own(core_at, bias, qc_own, r6, state[0], state[1], gain, terms, back)
    pieces = lax.all_to_all(terms.reshape(groups * shards, -1), AXES, 0, 0, tiled=True)
    return attended, jnp.sum(pieces, axis=0)


def solution(mesh):
    placed = (
        P(AXES, None),
        P(AXES, None),
        P(AXES, None),
        P("dp", None),
        P("dp", None, None),
        P("dp", None, None),
        P(),
        P(AXES, None),
    )
    return jax.shard_map(local, mesh=mesh, in_specs=placed, out_specs=(P(AXES, None), P(AXES)), check_vma=False)
```

time: 215 us -> 119 us (0.55)
  blocking collectives: 84.3 us -> 31.7 us
  Pallas kernels: 0 us -> 47.9 us
  local copies, waits for them, and re-layouts: 33.8 us -> 4.02 us
  matrix products: 24.3 us -> 0 us
  waiting for transfers between devices: 35.2 us -> 18.4 us
  starting transfers between devices: 23.4 us -> 13.1 us
  other arithmetic: 7.07 us -> 1.32 us
  between operations: 5.64 us -> 0.73 us
    unnamed x1 -> x0, blocking collectives: 84.3 us -> none
    pallas_call x0 -> x8, Pallas kernels: none -> 47.9 us  [the longest x2 17.9 us: middle(): pl.pallas_call(middle_kernel, grid=(PAIRS,), in_specs=[bias_at(4, place),...]
    all_to_all x0 -> x1, blocking collectives: none -> 31.7 us  [local(): lax.all_to_all(terms.reshape(groups * shards, -1), AXES, 0, 0, tiled=True)]
    dot_general x14 -> x0, matrix products: 24.3 us -> none  [the longest x7 16.8 us: absorb(): jnp.einsum('thd,uhd->htu', query_heads, keys_here, preferred_element_type...]
    ppermute x12 -> x0, local copies, waits for them, and re-layouts: 21.8 us -> none  [from_behind(): lax.ppermute(shard, axis, [(i, (i + by) % peers) for i in range(peers)])]
    ppermute x14 -> x9, waiting for transfers between devices: 35.2 us -> 18.4 us  [local(): move = lambda value, pairs: lax.ppermute(value, AXES, pairs)]
    ppermute x14 -> x9, starting transfers between devices: 23.4 us -> 13.1 us  [local(): move = lambda value, pairs: lax.ppermute(value, AXES, pairs)]
    unnamed x43 -> x21, local copies, waits for them, and re-layouts: 7.78 us -> 2.4 us
  transfers between devices with their start and end apart: 14 -> 9, of which waited for: 4 -> 6; matrix products, arithmetic and copies ran while one was open for 26% -> 2% of each run, Pallas kernels for 0% -> 33%
where the time goes in v1:
time: 119 us; the launch traced here: 117 us
  Pallas kernels  47.9 us (40%)
  blocking collectives  31.7 us (27%)
  waiting for transfers between devices  18.4 us (15%)
  starting transfers between devices  13.1 us (11%)
  local copies, waits for them, and re-layouts  4.02 us (3%)
  other arithmetic  1.32 us (1%)
    all_to_all x1, blocking collectives, local(): lax.all_to_all(terms.reshape(groups * shards, -1), AXES, 0, 0, tiled=True)  31.7 us
    ppermute x9, waiting for transfers between devices, local(): move = lambda value, pairs: lax.ppermute(value, AXES, pairs)  18.4 us
    pallas_call x2, Pallas kernels, middle(): pl.pallas_call(middle_kernel, grid=(PAIRS,), in_specs=[bias_at(4, place),...  17.9 us
    ppermute x9, starting transfers between devices, local(): move = lambda value, pairs: lax.ppermute(value, AXES, pairs)  13.1 us
    pallas_call x1, Pallas kernels, first(): pl.pallas_call(first_kernel, grid=(PAIRS,), in_specs=[bias_at(4, 0), COLS...  8.47 us
    pallas_call x1, Pallas kernels, last_own(): pl.pallas_call(own_kernel, grid_spec=pltpu.PrefetchScalarGridSpec(num_sca...  7.09 us
    pallas_call x1, Pallas kernels, last_sib(): pl.pallas_call(sib_kernel, grid_spec=pltpu.PrefetchScalarGridSpec(num_sca...  7.03 us
    pallas_call x2, Pallas kernels, split_heads(): pl.pallas_call(prep_kernel, grid_spec=pltpu.PrefetchScalarGridSpec(num_sc...  4.47 us
  transfers between devices with their start and end apart: 9, of which 6 were waited for; matrix products, arithmetic and copies ran while one was open for 2% of the time, Pallas kernels for 33%

profile of v1, /device:TPU:1, one launch (start us, length us, event | category | flops | bytes accessed | tf_op | source)
XLA Modules:
  0.0 117.1 jit_solution(15749728084343257951)
XLA Ops:
  0.6 2.2 %shard_map.97 = (bf16[256,1024]{1,0:T(8,128)(2,1)}, bf16[256,1024]{1,0:T(8,128)(2,1)}) custom-call(s32[1]{0:T(128)} %bitcast.core_ref, bf16[128,2048]{1,0:T(8,128)(2,1)} %a_other.3, bf16[128,2048]{1,0:T(8,128)(2,1)} %b_other.3, bf16[128,2048]{1,0:T(8,128)(2,1)} %a_other.3, bf16[128,2048]{1,0:T(8,128)(2,1)} %b_other.3), custom_call_target="tpu_custom_call" | custom-call | bytes 4194304 | tf_op jit(solution)/shard_map/pallas_call | solution.py:35
  2.8 3.2 %collective-permute-start = (bf16[256,1024]{1,0:T(8,128)(2,1)}, bf16[256,1024]{1,0:T(8,128)(2,1)S(1)}, u32[]{:S(2)}, u32[]{:S(2)}) collective-permute-start(bf16[256,1024]{1,0:T(8,128)(2,1)} %get-tuple-element.27), channel_id=1, source_target_pairs={{0,1},{1,0},{2,3},{3,2},{4,5},{5,4},{6,7},{7,6},{8,9},{9,8},{10,11... | collective-permute-start | bytes 1572872 | tf_op jit(solution)/shard_map/ppermute | solution.py:298
  6.0 1.7 %collective-permute-done.kv_b = bf16[256,1024]{1,0:T(8,128)(2,1)S(1)} collective-permute-done((bf16[256,1024]{1,0:T(8,128)(2,1)}, bf16[256,1024]{1,0:T(8,128)(2,1)S(1)}, u32[]{:S(2)}, u32[]{:S(2)}) %collective-permute-start) | collective-permute-done | bytes 524320 | tf_op jit(solution)/shard_map/ppermute | solution.py:298
  8.2 7.6 %collective-permute-done.2.kv_a = bf16[256,1024]{1,0:T(8,128)(2,1)S(1)} collective-permute-done((bf16[256,1024]{1,0:T(8,128)(2,1)}, bf16[256,1024]{1,0:T(8,128)(2,1)S(1)}, u32[]{:S(2)}, u32[]{:S(2)}) %collective-permute-start.2) | collective-permute-done | bytes 524320 | tf_op jit(solution)/shard_map/ppermute | solution.py:298
  15.8 4.4 %collective-permute-start.6 = (bf16[256,1024]{1,0:T(8,128)(2,1)}, bf16[256,1024]{1,0:T(8,128)(2,1)S(1)}, u32[]{:S(2)}, u32[]{:S(2)}) collective-permute-start(bf16[256,1024]{1,0:T(8,128)(2,1)} %get-tuple-element.32.kv_a), channel_id=1, source_target_pairs={{1,0},{3,1},{0,2},{5,3},{2,4},{7,5},{4,6},{9,7},{6,8},{11,9},{8,10... | collective-permute-start | bytes 1572872 | tf_op jit(solution)/shard_map/ppermute | solution.py:298
  20.5 2.3 %shard_map.96 = (bf16[256,1024]{1,0:T(8,128)(2,1)}, bf16[256,1024]{1,0:T(8,128)(2,1)}) custom-call(s32[1]{0:T(128)} %bitcast.core_ref, bf16[128,2048]{1,0:T(8,128)(2,1)} %a_other.2, bf16[128,2048]{1,0:T(8,128)(2,1)} %b_other.2, bf16[128,2048]{1,0:T(8,128)(2,1)} %a_other.2, bf16[128,2048]{1,0:T(8,128)(2,1)} %b_other.2), custom_call_target="tpu_custom_call" | custom-call | bytes 4194304 | tf_op jit(solution)/shard_map/pallas_call | solution.py:35
  23.2 6.1 %collective-permute-done.6.kv_a = bf16[256,1024]{1,0:T(8,128)(2,1)S(1)} collective-permute-done((bf16[256,1024]{1,0:T(8,128)(2,1)}, bf16[256,1024]{1,0:T(8,128)(2,1)S(1)}, u32[]{:S(2)}, u32[]{:S(2)}) %collective-permute-start.6) | collective-permute-done | bytes 524320 | tf_op jit(solution)/shard_map/ppermute | solution.py:298
  29.4 0.7 copy.12
  30.1 0.7 reshape.18.keep_ref
  30.8 1.3 %collective-permute-done.3.kv = bf16[256,1024]{1,0:T(8,128)(2,1)S(1)} collective-permute-done((bf16[256,1024]{1,0:T(8,128)(2,1)S(1)}, bf16[256,1024]{1,0:T(8,128)(2,1)S(1)}, u32[]{:S(2)}, u32[]{:S(2)}) %collective-permute-start.3) | collective-permute-done | bytes 524320 | tf_op jit(solution)/shard_map/ppermute | solution.py:298
  32.1 2.3 %collective-permute-start.4 = (bf16[256,1024]{1,0:T(8,128)(2,1)S(1)}, bf16[256,1024]{1,0:T(8,128)(2,1)S(1)}, u32[]{:S(2)}, u32[]{:S(2)}) collective-permute-start(bf16[256,1024]{1,0:T(8,128)(2,1)S(1)} %collective-permute-done.1.kv_b), channel_id=1, source_target_pairs={{1,0},{3,1},{0,2},{5,3},{2,4},{7,5},{4,6},{9,7},{6,8},{11,9},{8,10... | collective-permute-start | bytes 1572872 | tf_op jit(solution)/shard_map/ppermute | solution.py:298
  35.0 3.0 %shard_map.95.bias_ref = f32[1792,128]{1,0:T(8,128)} custom-call(s32[8]{0:T(128)} %and_select_fusion.blocks_ref, s32[1024]{0:T(1024)} %reshape.18.keep_ref, s32[1,4096]{1,0:T(1,128)} %docs_ref.1, s32[32,8]{1,0:T(8,128)} %bitcast.11), custom_call_target="tpu_custom_call" | custom-call | flops 1048576 | bytes 2097152 | tf_op jit(solution)/shard_map/pallas_call | solution.py:92
  38.0 0.8 copy-done
  38.8 8.5 %shard_map.98 = (f32[64,256]{1,0:T(8,128)}, f32[1024,128]{1,0:T(8,128)}, f32[64,256]{1,0:T(8,128)}, f32[1024,128]{1,0:T(8,128)}) custom-call(f32[1792,128]{1,0:T(8,128)} %shard_map.95.bias_ref, bf16[256,1024]{1,0:T(8,128)(2,1)} %get-tuple-element.26.qc_own.qc, bf16[256,1024]{1,0:T(8,128)(2,1)} %copy-done, bf16[256,1024]{1,0:T(8,128)(2,1)} %get-tuple-element.32.kv_a, ...), custom_call_target="tpu_custom_call" | custom-call | flops 268435456 | bytes 4194304 | tf_op jit(solution)/shard_map/pallas_call | solution.py:205
  47.2 8.9 %shard_map.99 = (f32[64,256]{1,0:T(8,128)}, f32[1024,128]{1,0:T(8,128)}, f32[64,256]{1,0:T(8,128)}, f32[1024,128]{1,0:T(8,128)}) custom-call(f32[1792,128]{1,0:T(8,128)} %shard_map.95.bias_ref, bf16[256,1024]{1,0:T(8,128)(2,1)} %get-tuple-element.26.qc_own.qc, bf16[256,1024]{1,0:T(8,128)(2,1)} %copy-done, bf16[256,1024]{1,0:T(8,128)(2,1)} %copy-done.5, ...), custom_call_target="tpu_custom_call" | custom-call | flops 268435456 | bytes 4194304 | tf_op jit(solution)/shard_map/pallas_call | solution.py:216
  56.2 8.9 %shard_map.100 = (f32[64,256]{1,0:T(8,128)}, f32[1024,128]{1,0:T(8,128)}, f32[64,256]{1,0:T(8,128)}, f32[1024,128]{1,0:T(8,128)}) custom-call(f32[1792,128]{1,0:T(8,128)} %shard_map.95.bias_ref, bf16[256,1024]{1,0:T(8,128)(2,1)} %get-tuple-element.26.qc_own.qc, bf16[256,1024]{1,0:T(8,128)(2,1)} %copy-done, bf16[256,1024]{1,0:T(8,128)(2,1)} %copy-done.6, ...), custom_call_target="tpu_custom_call" | custom-call | flops 268435456 | bytes 4194304 | tf_op jit(solution)/shard_map/pallas_call | solution.py:216
  65.1 7.0 %shard_map.101 = (bf16[128,1024]{1,0:T(8,128)(2,1)}, f32[64,128]{1,0:T(8,128)}) custom-call(s32[1]{0:T(128)} %bitcast.core_ref, f32[1792,128]{1,0:T(8,128)} %shard_map.95.bias_ref, bf16[256,1024]{1,0:T(8,128)(2,1)} %copy-done, bf16[256,1024]{1,0:T(8,128)(2,1)} %copy-done.2, f32[64,256]{1,0:T(8,128)} %get-tuple-element.44.rows, ...), custom_call_target="tpu_custom_call" | custom-call | flops 67108864 | bytes 4194304 | tf_op jit(solution)/shard_map/pallas_call | solution.py:227
  72.2 2.3 %collective-permute-start.8 = (bf16[128,1024]{1,0:T(8,128)(2,1)}, bf16[128,1024]{1,0:T(8,128)(2,1)S(1)}, u32[]{:S(2)}, u32[]{:S(2)}) collective-permute-start(bf16[128,1024]{1,0:T(8,128)(2,1)} %get-tuple-element.47), channel_id=1, source_target_pairs={{0,1},{1,0},{2,3},{3,2},{4,5},{5,4},{6,7},{7,6},{8,9},{9,8},{10,11... | collective-permute-start | bytes 786440 | tf_op jit(solution)/shard_map/ppermute | solution.py:298
  74.5 1.4 %collective-permute-done.8.back = bf16[128,1024]{1,0:T(8,128)(2,1)S(1)} collective-permute-done((bf16[128,1024]{1,0:T(8,128)(2,1)}, bf16[128,1024]{1,0:T(8,128)(2,1)S(1)}, u32[]{:S(2)}, u32[]{:S(2)}) %collective-permute-start.8) | collective-permute-done | bytes 262176 | tf_op jit(solution)/shard_map/ppermute | solution.py:298
  75.9 0.7 copy-done.7
  76.8 7.1 %shard_map.102 = (bf16[128,2048]{1,0:T(8,128)(2,1)}, f32[16,128]{1,0:T(8,128)}) custom-call(s32[1]{0:T(128)} %bitcast.core_ref, f32[1792,128]{1,0:T(8,128)} %shard_map.95.bias_ref, bf16[256,1024]{1,0:T(8,128)(2,1)} %get-tuple-element.26.qc_own.qc, bf16[256,1024]{1,0:T(8,128)(2,1)} %copy-done.3, f32[64,256]{1,0:T(8,128)} %get-tuple-element.42.rows, ...), custom_call_target="tpu_custom_call" | custom-call | flops 67108864 | bytes 4194304 | tf_op jit(solution)/shard_map/pallas_call | solution.py:244
  83.9 0.8 all_to_all.6
  84.7 31.7 %all_to_all.9 = f32[256,1,8]{2,1,0:T(1,128)S(1)} all-to-all(f32[256,1,8]{2,1,0:T(1,128)S(1)} %bitcast.10), channel_id=1, replica_groups=mesh['dp'=8,'seq'=32] {'dp','seq'}, dimensions={0} | all-to-all | bytes 16384 | tf_op jit(solution)/shard_map/all_to_all | solution.py:320
  116.3 0.8 reduce_sum.9
  (30 shorter events, 2.0 us)
Async XLA Ops:
  2.8 5.0 %collective-permute-start = (bf16[256,1024]{1,0:T(8,128)(2,1)}, bf16[256,1024]{1,0:T(8,128)(2,1)S(1)}, u32[]{:S(2)}, u32[]{:S(2)}) collective-permute-start(bf16[256,1024]{1,0:T(8,128)(2,1)} %get-tuple-element.27), channel_id=1, source_target_pairs={{0,1},{1,0},{2,3},{3,2},{4,5},{5,4},{6,7},{7,6},{8,9},{9,8},{10,11... | collective-permute-start | bytes 1572872 | tf_op jit(solution)/shard_map/ppermute | solution.py:298
  6.0 9.7 %collective-permute-start.2 = (bf16[256,1024]{1,0:T(8,128)(2,1)}, bf16[256,1024]{1,0:T(8,128)(2,1)S(1)}, u32[]{:S(2)}, u32[]{:S(2)}) collective-permute-start(bf16[256,1024]{1,0:T(8,128)(2,1)} %get-tuple-element.32.kv_a), channel_id=1, source_target_pairs={{0,1},{1,3},{2,0},{3,5},{4,2},{5,7},{6,4},{7,9},{8,6},{9,11},{10,8... | collective-permute-start | bytes 1572872 | tf_op jit(solution)/shard_map/ppermute | solution.py:298
  7.8 21.4 %copy-start.1 = (bf16[256,1024]{1,0:T(8,128)(2,1)}, bf16[256,1024]{1,0:T(8,128)(2,1)S(1)}, u32[]{:S(2)}) copy-start(bf16[256,1024]{1,0:T(8,128)(2,1)S(1)} %collective-permute-done.kv_b) | copy-start | bytes 1572868
  7.8 12.7 %collective-permute-start.1 = (bf16[256,1024]{1,0:T(8,128)(2,1)S(1)}, bf16[256,1024]{1,0:T(8,128)(2,1)S(1)}, u32[]{:S(2)}, u32[]{:S(2)}) collective-permute-start(bf16[256,1024]{1,0:T(8,128)(2,1)S(1)} %collective-permute-done.kv_b), channel_id=1, source_target_pairs={{1,0},{3,1},{0,2},{5,3},{2,4},{7,5},{4,6},{9,7},{6,8},{11,9},{8,10... | collective-permute-start | bytes 1572872 | tf_op jit(solution)/shard_map/ppermute | solution.py:298
  15.8 7.0 %copy-start.5 = (bf16[256,1024]{1,0:T(8,128)(2,1)}, bf16[256,1024]{1,0:T(8,128)(2,1)S(1)}, u32[]{:S(2)}) copy-start(bf16[256,1024]{1,0:T(8,128)(2,1)S(1)} %collective-permute-done.2.kv_a) | copy-start | bytes 1572868
  15.8 13.5 %collective-permute-start.6 = (bf16[256,1024]{1,0:T(8,128)(2,1)}, bf16[256,1024]{1,0:T(8,128)(2,1)S(1)}, u32[]{:S(2)}, u32[]{:S(2)}) collective-permute-start(bf16[256,1024]{1,0:T(8,128)(2,1)} %get-tuple-element.32.kv_a), channel_id=1, source_target_pairs={{1,0},{3,1},{0,2},{5,3},{2,4},{7,5},{4,6},{9,7},{6,8},{11,9},{8,10... | collective-permute-start | bytes 1572872 | tf_op jit(solution)/shard_map/ppermute | solution.py:298
  20.4 11.7 %copy-start.4 = (bf16[256,1024]{1,0:T(8,128)(2,1)}, bf16[256,1024]{1,0:T(8,128)(2,1)S(1)}, u32[]{:S(2)}) copy-start(bf16[256,1024]{1,0:T(8,128)(2,1)S(1)} %collective-permute-done.1.kv_b) | copy-start | bytes 1572868
  20.4 11.7 %collective-permute-start.3 = (bf16[256,1024]{1,0:T(8,128)(2,1)S(1)}, bf16[256,1024]{1,0:T(8,128)(2,1)S(1)}, u32[]{:S(2)}, u32[]{:S(2)}) collective-permute-start(bf16[256,1024]{1,0:T(8,128)(2,1)S(1)} %collective-permute-done.2.kv_a), channel_id=1, source_target_pairs={{0,1},{1,3},{2,0},{3,5},{4,2},{5,7},{6,4},{7,9},{8,6},{9,11},{10,8... | collective-permute-start | bytes 1572872 | tf_op jit(solution)/shard_map/ppermute | solution.py:298
  20.5 8.9 %copy-start.9 = (s32[1,32,8]{1,2,0:T(8,128)S(1)}, s32[1,32,8]{1,2,0:T(8,128)}, u32[]{:S(2)}) copy-start(s32[1,32,8]{1,2,0:T(8,128)} %param.12) | copy-start | bytes 3076
  22.8 15.2 %collective-permute-start.5 = (bf16[256,1024]{1,0:T(8,128)(2,1)}, bf16[256,1024]{1,0:T(8,128)(2,1)S(1)}, u32[]{:S(2)}, u32[]{:S(2)}) collective-permute-start(bf16[256,1024]{1,0:T(8,128)(2,1)} %get-tuple-element.31), channel_id=1, source_target_pairs={{0,1},{1,0},{2,3},{3,2},{4,5},{5,4},{6,7},{7,6},{8,9},{9,8},{10,11... | collective-permute-start | bytes 1572872 | tf_op jit(solution)/shard_map/ppermute | solution.py:298
  29.2 1.6 %copy-start.6 = (bf16[256,1024]{1,0:T(8,128)(2,1)}, bf16[256,1024]{1,0:T(8,128)(2,1)S(1)}, u32[]{:S(2)}) copy-start(bf16[256,1024]{1,0:T(8,128)(2,1)S(1)} %collective-permute-done.6.kv_a) | copy-start | bytes 1572868
  29.2 26.9 %collective-permute-start.7 = (bf16[256,1024]{1,0:T(8,128)(2,1)S(1)}, bf16[256,1024]{1,0:T(8,128)(2,1)}, u32[]{:S(2)}, u32[]{:S(2)}) collective-permute-start(bf16[256,1024]{1,0:T(8,128)(2,1)S(1)} %collective-permute-done.kv_b), channel_id=1, source_target_pairs={{0,1},{1,3},{2,0},{3,5},{4,2},{5,7},{6,4},{7,9},{8,6},{9,11},{10,8... | collective-permute-start | bytes 1572872 | tf_op jit(solution)/shard_map/ppermute | solution.py:298
  29.3 0.8 copy-start.8
  32.1 15.1 %copy-start.2 = (bf16[256,1024]{1,0:T(8,128)(2,1)}, bf16[256,1024]{1,0:T(8,128)(2,1)S(1)}, u32[]{:S(2)}) copy-start(bf16[256,1024]{1,0:T(8,128)(2,1)S(1)} %collective-permute-done.3.kv) | copy-start | bytes 1572868
  32.1 43.8 %collective-permute-start.4 = (bf16[256,1024]{1,0:T(8,128)(2,1)S(1)}, bf16[256,1024]{1,0:T(8,128)(2,1)S(1)}, u32[]{:S(2)}, u32[]{:S(2)}) collective-permute-start(bf16[256,1024]{1,0:T(8,128)(2,1)S(1)} %collective-permute-done.1.kv_b), channel_id=1, source_target_pairs={{1,0},{3,1},{0,2},{5,3},{2,4},{7,5},{4,6},{9,7},{6,8},{11,9},{8,10... | collective-permute-start | bytes 1572872 | tf_op jit(solution)/shard_map/ppermute | solution.py:298
  38.0 0.8 copy-start
  72.2 3.7 %collective-permute-start.8 = (bf16[128,1024]{1,0:T(8,128)(2,1)}, bf16[128,1024]{1,0:T(8,128)(2,1)S(1)}, u32[]{:S(2)}, u32[]{:S(2)}) collective-permute-start(bf16[128,1024]{1,0:T(8,128)(2,1)} %get-tuple-element.47), channel_id=1, source_target_pairs={{0,1},{1,0},{2,3},{3,2},{4,5},{5,4},{6,7},{7,6},{8,9},{9,8},{10,11... | collective-permute-start | bytes 786440 | tf_op jit(solution)/shard_map/ppermute | solution.py:298
  75.9 0.7 copy-start.7
  75.9 0.9 copy-start.3
